TPU v7x, 256 devices: a whole 4x4x8 slice. The times are simulated.
256 devices in a mesh: query: 32 (over x, z_hi, y), entity: 8 (over z_lo, core).
Axes of the slice: x: 4, y: 4, z: 8 (z_hi: 2, z_lo: 4; z = z_hi * 4 + z_lo), core: 2. Of those that a mesh axis runs over, the one named last changes fastest.
Arguments:
- anchor_ids: int32 [16384], P('query'), may hold values from 0 to 32767
- relation_ids: int32 [16384], P('query'), may hold values from 0 to 4130
- side_flags: int32 [16384], P('query'), may hold values from 0 to 1
- teacher_entities: bfloat16 [32768, 1000], P(('entity', 'query')), may hold values from -1.2 to 1.2, as said below
- student_entities: bfloat16 [32768, 128], P(('entity', 'query')), may hold values from -2.1 to 2.1, as said below
- teacher_relations: bfloat16 [4131, 1000], replicated, may hold values from -9 to 33, as said below
- student_relations: bfloat16 [4131, 128], replicated, may hold values from -9 to 63.6875, as said below
Outputs:
- divergence: float32 [16384], P('query')
- entity_grad: float32 [32768, 128], P(('entity', 'query'))
- query_grad: float32 [16384, 128], P('query')
Inputs may be any that keep to these rules, and one draw needn't show every extreme that they name: `teacher_entities`: Real-valued embeddings. `student_entities`: Real-valued embeddings. `teacher_relations`: Real-valued embeddings. `student_relations`: Real-valued embeddings.
All inputs are finite; a program needn't handle non-finite values.
Results may differ from a plain program's by a relative error of at most 0.013.
Values may be sent and summed in bfloat16 or wider, within the bound.
A program may use at most 128 MiB of HBM per device.

v0:
```python
import jax
import jax.numpy as jnp
from jax import lax
from jax.sharding import PartitionSpec as P


def query_vectors(anchor, relation, flags):
    half = anchor.shape[1] // 2
    sign = (2 * flags - 1).astype(jnp.float32)[:, None]
    a_re = anchor[:, :half]
    a_im = anchor[:, half:]
    r_re = relation[:, :half]
    r_im = relation[:, half:]
    real = a_re * r_re - sign * a_im * r_im
    imag = a_im * r_re + sign * a_re * r_im
    return jnp.concatenate([real, imag], axis=1).astype(jnp.bfloat16)


def per_device(
    anchor_ids,
    relation_ids,
    side_flags,
    teacher_entities,
    student_entities,
    teacher_relations,
    student_relations,
):
    teacher_slab, student_slab = (
        lax.all_gather(teacher_entities, "query", axis=0, tiled=True),
        lax.all_gather(student_entities, "query", axis=0, tiled=True),
    )
    slab = teacher_slab.shape[0]
    offset = lax.axis_index("entity") * slab
    local = anchor_ids - offset
    inside = ((local >= 0) & (local < slab))[:, None]
    safe = jnp.clip(local, 0, slab - 1)
    teacher_part = jnp.where(inside, jnp.take(teacher_slab, safe, axis=0).astype(jnp.float32), 0.0)
    student_part = jnp.where(inside, jnp.take(student_slab, safe, axis=0).astype(jnp.float32), 0.0)
    teacher_anchor, student_anchor = (
        lax.psum(teacher_part.astype(jnp.bfloat16), "entity").astype(jnp.float32),
        lax.psum(student_part.astype(jnp.bfloat16), "entity").astype(jnp.float32),
    )
    query_teacher = query_vectors(
        teacher_anchor,
        jnp.take(teacher_relations, relation_ids, axis=0).astype(jnp.float32),
        side_flags,
    )
    query_student = query_vectors(
        student_anchor,
        jnp.take(student_relations, relation_ids, axis=0).astype(jnp.float32),
        side_flags,
    )
    rows = query_teacher.shape[0]
    block = 1024
    count = slab // block
    teacher_blocks = teacher_slab.reshape(count, block, teacher_slab.shape[1])
    student_blocks = student_slab.reshape(count, block, student_slab.shape[1])

    def first_pass(carry, items):
        top_t, total_t, weighted, top_s, total_s = carry
        t = jnp.dot(query_teacher, items[0].T, preferred_element_type=jnp.float32)
        s = jnp.dot(query_student, items[1].T, preferred_element_type=jnp.float32)
        new_t = jnp.maximum(top_t, jnp.max(t, axis=1))
        factor_t = jnp.exp(top_t - new_t)
        expo_t = jnp.exp(t - new_t[:, None])
        total_t = total_t * factor_t + jnp.sum(expo_t, axis=1)
        weighted = weighted * factor_t + jnp.sum(expo_t * (t - s), axis=1)
        new_s = jnp.maximum(top_s, jnp.max(s, axis=1))
        total_s = total_s * jnp.exp(top_s - new_s) + jnp.sum(jnp.exp(s - new_s[:, None]), axis=1)
        kept = None
        return ((new_t, total_t, weighted, new_s, total_s), kept)

    lowest = jnp.full((rows,), -jnp.inf, jnp.float32)
    nothing = jnp.zeros((rows,), jnp.float32)
    stats, kept = lax.scan(
        first_pass, (lowest, nothing, nothing, lowest, nothing), (teacher_blocks, student_blocks)
    )
    top_t, total_t, weighted, top_s, total_s = stats
    best_t, best_s = lax.pmax((top_t, top_s), "entity")
    factor_t = jnp.exp(top_t - best_t)
    factor_s = jnp.exp(top_s - best_s)
    total_t, weighted, total_s = lax.psum(
        (total_t * factor_t, weighted * factor_t, total_s * factor_s), "entity"
    )
    top_t, top_s = (best_t, best_s)
    divergence = weighted / total_t - top_t - jnp.log(total_t) + top_s + jnp.log(total_s)

    def second_pass(q_grad, items):
        t = jnp.dot(query_teacher, items[0].T, preferred_element_type=jnp.float32)
        s = jnp.dot(query_student, items[1].T, preferred_element_type=jnp.float32)
        prob_t = jnp.exp(t - top_t[:, None]) / total_t[:, None]
        prob_s = jnp.exp(s - top_s[:, None]) / total_s[:, None]
        weights = (prob_s - prob_t).astype(jnp.bfloat16)
        grad_block = jnp.dot(weights.T, query_student, preferred_element_type=jnp.float32)
        q_grad = q_grad + jnp.dot(weights, items[1], preferred_element_type=jnp.float32)
        return (q_grad, grad_block)

    start = jnp.zeros((rows, query_student.shape[1]), jnp.float32)
    q_grad, grad_blocks = lax.scan(second_pass, start, (teacher_blocks, student_blocks))
    slab_grad = grad_blocks.reshape(slab, query_student.shape[1])
    entity_grad = lax.psum_scatter(slab_grad, "query", scatter_dimension=0, tiled=True)
    query_grad = lax.psum(q_grad, "entity")
    return (divergence, entity_grad, query_grad)


def solution(mesh):
    in_specs = (
        P("query"),
        P("query"),
        P("query"),
        P(("entity", "query"), None),
        P(("entity", "query"), None),
        P(),
        P(),
    )
    out_specs = (P("query"), P(("entity", "query"), None), P("query", None))
    return jax.shard_map(
        per_device, mesh=mesh, in_specs=in_specs, out_specs=out_specs, check_vma=False
    )
```

profile of v0, /device:TPU:32, one launch (start us, length us, event | category | flops | bytes accessed | tf_op | source)
XLA Modules:
  0.0 744.2 jit_solution(13715478936245018552)
XLA Ops:
  8.0 1.8 copy.10
  10.6 83.7 %all-gather.5.cloned.1.call-done = bf16[4096,128]{1,0:T(8,128)(2,1)} async-done(((bf16[128,128]{1,0:T(8,128)(2,1)}), bf16[4096,128]{1,0:T(8,128)(2,1)}) %all-gather.5.cloned.1.call-update) | async-done | bytes 1048592 | tf_op jit(solution)/shard_map/all_gather | solution.py:30
  94.3 2.4 gather_fusion.2
  97.5 149.9 %all-gather.3.cloned.1.call-done = bf16[4096,1000]{1,0:T(8,128)(2,1)} async-done(((bf16[128,1000]{1,0:T(8,128)(2,1)}), bf16[4096,1000]{1,0:T(8,128)(2,1)}) %all-gather.3.cloned.1.call-update) | async-done | bytes 8192016 | tf_op jit(solution)/shard_map/all_gather | solution.py:29
  247.4 7.2 gather_fusion
  256.1 12.1 %copy.11 = bf16[4131,1000]{1,0:T(8,128)(2,1)} copy(bf16[4131,1000]{0,1:T(8,128)(2,1)} %param.16) | data formatting | bytes 16524000 | tf_op args[5]
  268.3 8.0 %gather_fusion.1 = bf16[512,1000]{1,0:T(8,128)(2,1)} fusion(bf16[4131,1000]{1,0:T(8,128)(2,1)} %copy.11, s32[1024]{0:T(1024)S(1)} %pad_clamp_fusion), kind=kCustom, calls=%fused_computation.1 | custom fusion | bytes 2050048 | tf_op jit(solution)/shard_map/jit(_take)/gather | solution.py:45
  280.6 43.3 %all-reduce.8.cloned.1.call-done = (bf16[512,1000]{1,0:T(8,128)(2,1)}, bf16[512,128]{1,0:T(8,128)(2,1)}) async-done(((bf16[512,1000]{1,0:T(8,128)(2,1)}, bf16[512,128]{1,0:T(8,128)(2,1)}), (bf16[512,1000]{1,0:T(8,128)(2,1)}, bf16[512,128]{1,0:T(8,128)(2,1)})) %all-reduce.8.cloned.1.call-update) | async-done | bytes 1155088 | tf_op jit(solution)/shard_map/psum | solution.py:40
  323.9 1.5 convert_element_type.33
  328.1 46.0 %while.32 = (s32[]{:T(128)}, f32[512]{0:T(512)S(1)}, f32[512]{0:T(512)}, f32[512]{0:T(512)}, f32[512]{0:T(512)}, /*index=5*/f32[512]{0:T(512)}, bf16[4,1024,1000...) while((s32[]{:T(128)}, f32[512]{0:T(512)S(1)}, ...), condition=%wide.region_8.9_spmd.clone, body=%wide.region_2.8_spmd.clone.sunk | while | flops 1187518464 | bytes 12046677 | solution.py:75
  328.1 5.1 fusion.51
  333.2 2.0 fusion.52
  336.6 2.4 multiply_reduce_fusion.2
  339.6 5.1 fusion.51
  344.7 2.0 fusion.52
  348.1 2.4 multiply_reduce_fusion.2
  351.2 5.1 fusion.51
  356.2 2.0 fusion.52
  359.6 2.4 multiply_reduce_fusion.2
  362.7 5.1 fusion.51
  367.7 2.0 fusion.52
  371.1 2.4 multiply_reduce_fusion.2
  374.2 14.8 %all-reduce.1 = (f32[512]{0:T(512)}, f32[512]{0:T(512)}) all-reduce(f32[512]{0:T(512)} %get-tuple-element.120, f32[512]{0:T(512)S(1)} %get-tuple-element.118), channel_id=1, replica_groups=mesh['query'=32,'entity'=8] {'entity'}, use_global_device_ids=true, to_apply=%region_12.13 | all-reduce | flops 1024 | bytes 8192 | tf_op jit(solution)/shard_map/pmax | solution.py:79
  389.7 14.6 %all-reduce = (f32[512]{0:T(512)S(1)}, f32[512]{0:T(512)}, f32[512]{0:T(512)}) all-reduce(f32[512]{0:T(512)S(1)} %get-tuple-element.261, f32[512]{0:T(512)S(1)} %get-tuple-element.259, f32[512]{0:T(512)S(1)} %get-tuple-element.258), channel_id=1, replica_groups=mesh['query'=32,'entity'=8] {'entity'}, use_global_device_ids=true, to_apply=%region_13.14 | all-reduce | flops 1536 | bytes 12288 | tf_op jit(solution)/shard_map/psum | solution.py:82
  404.3 26.0 %while.33 = (s32[]{:T(128)}, f32[512,128]{1,0:T(8,128)S(1)}, f32[4,1024,128]{2,1,0:T(8,128)}, bf16[4,1024,128]{2,1,0:T(8,128)(2,1)}, bf16[512,128]{1,0:T(8,128)(...) while((s32[]{:T(128)}, f32[512,128]{1,0:T(8,128)S(1)}, ...), condition=%wide.region_15.16_spmd.clone, body=%wide.region_14.15_spmd.clone.sunk | while | flops 1454505984 | bytes 16531671 | solution.py:99
  404.3 3.2 fusion.62
  410.8 3.2 fusion.62
  417.3 3.2 fusion.62
  423.8 3.2 fusion.62
  432.9 69.5 %all-reduce.6.cloned.1.call-done = f32[512,128]{1,0:T(8,128)} async-done(((f32[512,128]{1,0:T(8,128)}), f32[512,128]{1,0:T(8,128)}) %all-reduce.6.cloned.1.call-update) | async-done | bytes 262160 | tf_op jit(solution)/shard_map/psum | solution.py:102
  502.4 233.6 %reduce-scatter.2.cloned.1.call-done = f32[128,128]{1,0:T(8,128)} async-done(((f32[4096,128]{1,0:T(8,128)}), f32[128,128]{1,0:T(8,128)}) %reduce-scatter.2.cloned.1.call-update) | async-done | bytes 65552 | tf_op jit(solution)/shard_map/reduce_scatter | solution.py:101
  736.0 1.7 copy.43
  (157 shorter events, 34.9 us)
Async XLA Ops:
  7.2 269.1 %copy-start = (bf16[4131,128]{1,0:T(8,128)(2,1)S(1)}, bf16[4131,128]{1,0:T(8,128)(2,1)}, u32[]{:S(2)}) copy-start(bf16[4131,128]{1,0:T(8,128)(2,1)} %param.17) | copy-start | bytes 3172612
  7.2 87.1 %all-gather.5.cloned.1.call-start = ((), (), s32[]{:S(2)}) async-start(), calls=%async_computation.2 | async-start | bytes 1081344 | tf_op jit(solution)/shard_map/all_gather | solution.py:30
  7.9 239.5 %all-gather.3.cloned.1.call-start = ((), (), s32[]{:S(2)}) async-start(), calls=%async_computation.1 | async-start | bytes 8650752 | tf_op jit(solution)/shard_map/all_gather | solution.py:29
  9.8 314.0 %all-reduce.8.cloned.1.call-start = ((), (), s32[]{:S(2)}) async-start(), calls=%async_computation.5 | async-start | bytes 2359296 | tf_op jit(solution)/shard_map/psum | solution.py:40
  256.0 246.4 %all-reduce.6.cloned.1.call-start = ((), (), s32[]{:S(2)}) async-start(), calls=%async_computation.4 | async-start | bytes 524288 | tf_op jit(solution)/shard_map/psum | solution.py:102
  268.3 9.4 %copy-start.14 = (s32[512]{0:T(512)S(1)}, s32[512]{0:T(512)}, u32[]{:S(2)}) copy-start(s32[512]{0:T(512)} %param.13) | copy-start | bytes 6148
  323.9 1.5 copy-start.12
  336.5 2.4 copy-start.4
  336.5 2.4 copy-start.6
  336.5 2.4 copy-start.8
  336.6 2.4 copy-start.10
  348.1 2.4 copy-start.4
  348.1 2.4 copy-start.6
  348.1 2.4 copy-start.8
  348.1 2.4 copy-start.10
  359.6 2.4 copy-start.4
  359.6 2.4 copy-start.6
  359.6 2.4 copy-start.8
  359.6 2.4 copy-start.10
  371.1 2.4 copy-start.4
  371.1 2.4 copy-start.6
  371.1 2.4 copy-start.8
  371.1 2.4 copy-start.10
  404.3 3.2 copy-start.1
  404.3 3.2 copy-start.15
  410.8 3.2 copy-start.1
  410.8 3.2 copy-start.15
  417.3 3.2 copy-start.1
  417.3 3.2 copy-start.15
  423.8 3.2 copy-start.1
  423.8 3.2 copy-start.15
  431.0 305.0 %reduce-scatter.2.cloned.1.call-start = ((), (), s32[]{:S(2)}) async-start(), calls=%async_computation.3 | async-start | bytes 2162688 | tf_op jit(solution)/shard_map/reduce_scatter | solution.py:101
  (18 other events, 15.1 us)
Sparse Core Ops, SparseCore 0:
  11.4 82.7 all-gather.4
  98.4 149.0 all-gather.2
  256.1 67.6 all-reduce.7
  431.1 71.2 all-reduce.5
  505.5 230.4 reduce-scatter.1
where the time goes:
time: 745 us; the launch traced here: 744 us
  waiting for transfers between devices  581 us (78%)
  matrix products  53.9 us (7%)
  local copies, waits for them, and re-layouts  37.8 us (5%)
  blocking collectives  29.4 us (4%)
  other arithmetic  27 us (4%)
  between operations  14 us (2%)
    reduce_scatter x1, waiting for transfers between devices, per_device(): lax.psum_scatter(slab_grad, 'query', scatter_dimension=0, tiled=True)  234 us
    all_gather x1, waiting for transfers between devices, per_device(): lax.all_gather(teacher_entities, 'query', axis=0, tiled=True)  150 us
    all_gather x1, waiting for transfers between devices, per_device(): lax.all_gather(student_entities, 'query', axis=0, tiled=True)  83.7 us
    psum x1, waiting for transfers between devices, per_device(): query_grad = lax.psum(q_grad, 'entity')  69.5 us
    psum x1, waiting for transfers between devices, per_device(): lax.psum(teacher_part.astype(jnp.bfloat16), 'entity').astype(jnp.float32)  43.3 us
    dot_general x4, matrix products, first_pass(): t = jnp.dot(query_teacher, items[0].T, preferred_element_type=jnp.float32)  20.3 us
    unnamed x21, local copies, waits for them, and re-layouts  16.4 us
  transfers between devices with their start and end apart: 5, of which 5 were waited for; matrix products, arithmetic and copies ran while one was open for 4% of the time, Pallas kernels for 0%

commit v1 on v0

--- a/solution.py
+++ b/solution.py
@@ -36,8 +36,9 @@
     safe = jnp.clip(local, 0, slab - 1)
     teacher_part = jnp.where(inside, jnp.take(teacher_slab, safe, axis=0).astype(jnp.float32), 0.0)
     student_part = jnp.where(inside, jnp.take(student_slab, safe, axis=0).astype(jnp.float32), 0.0)
+    raise_zone = lambda xx: lax.all_gather(xx, "entity").sum(axis=0)
     teacher_anchor, student_anchor = (
-        lax.psum(teacher_part.astype(jnp.bfloat16), "entity").astype(jnp.float32),
+        raise_zone(teacher_part.astype(jnp.bfloat16)).astype(jnp.float32),
         lax.psum(student_part.astype(jnp.bfloat16), "entity").astype(jnp.float32),
     )
     query_teacher = query_vectors(

time: 745 us -> 834 us (1.12)
  waiting for transfers between devices: 581 us -> 659 us
    all_gather x0 -> x1, waiting for transfers between devices: none -> 89.3 us  [per_device(): raise_zone = lambda xx: lax.all_gather(xx, 'entity').sum(axis=0)]
    psum x1, waiting for transfers between devices: 43.3 us -> 31.5 us  [per_device(): lax.psum(student_part.astype(jnp.bfloat16), 'entity').astype(jnp.float32)]
  transfers between devices with their start and end apart: 5 -> 6, of which waited for: 5 -> 6; matrix products, arithmetic and copies ran while one was open for 4% -> 5% of each run, Pallas kernels for 0% -> 0%
where the time goes in v1:
time: 834 us; the launch traced here: 833 us
  waiting for transfers between devices  659 us (79%)
  matrix products  54 us (6%)
  local copies, waits for them, and re-layouts  40.8 us (5%)
  other arithmetic  34.7 us (4%)
  blocking collectives  29.1 us (3%)
  between operations  14.3 us (2%)
    reduce_scatter x1, waiting for transfers between devices, per_device(): lax.psum_scatter(slab_grad, 'query', scatter_dimension=0, tiled=True)  233 us
    all_gather x1, waiting for transfers between devices, per_device(): lax.all_gather(teacher_entities, 'query', axis=0, tiled=True)  150 us
    all_gather x1, waiting for transfers between devices, per_device(): raise_zone = lambda xx: lax.all_gather(xx, 'entity').sum(axis=0)  89.3 us
    all_gather x1, waiting for transfers between devices, per_device(): lax.all_gather(student_entities, 'query', axis=0, tiled=True)  83.7 us
    psum x1, waiting for transfers between devices, per_device(): query_grad = lax.psum(q_grad, 'entity')  70.9 us
    psum x1, waiting for transfers between devices, per_device(): lax.psum(student_part.astype(jnp.bfloat16), 'entity').astype(jnp.float32)  31.5 us
    dot_general x4, matrix products, first_pass(): t = jnp.dot(query_teacher, items[0].T, preferred_element_type=jnp.float32)  20.2 us
  transfers between devices with their start and end apart: 6, of which 6 were waited for; matrix products, arithmetic and copies ran while one was open for 5% of the time, Pallas kernels for 0%

profile of v1, /device:TPU:32, one launch (start us, length us, event | category | flops | bytes accessed | tf_op | source)
XLA Modules:
  0.0 833.1 jit_solution(13549640939313955465)
XLA Ops:
  10.6 83.7 %all-gather.8.cloned.1.call-done = bf16[4096,128]{1,0:T(8,128)(2,1)} async-done(((bf16[128,128]{1,0:T(8,128)(2,1)}), bf16[4096,128]{1,0:T(8,128)(2,1)}) %all-gather.8.cloned.1.call-update) | async-done | bytes 1048592 | tf_op jit(solution)/shard_map/all_gather | solution.py:30
  94.3 2.4 gather_fusion.2
  97.6 149.8 %all-gather.4.cloned.1.call-done = bf16[4096,1000]{1,0:T(8,128)(2,1)} async-done(((bf16[128,1000]{1,0:T(8,128)(2,1)}), bf16[4096,1000]{1,0:T(8,128)(2,1)}) %all-gather.4.cloned.1.call-update) | async-done | bytes 8192016 | tf_op jit(solution)/shard_map/all_gather | solution.py:29
  247.4 7.2 gather_fusion
  256.8 12.2 %copy.22 = bf16[4131,1000]{1,0:T(8,128)(2,1)} copy(bf16[4131,1000]{0,1:T(8,128)(2,1)} %param.16) | data formatting | bytes 16524000 | tf_op args[5]
  269.1 8.0 gather_fusion.1
  281.3 31.5 %all-reduce.5.cloned.1.call-done = bf16[512,128]{1,0:T(8,128)(2,1)} async-done(((bf16[512,128]{1,0:T(8,128)(2,1)}), bf16[512,128]{1,0:T(8,128)(2,1)}) %all-reduce.5.cloned.1.call-update) | async-done | bytes 131088 | tf_op jit(solution)/shard_map/psum | solution.py:42
  315.2 89.3 %all-gather.6.cloned.1.call-done = bf16[8,512,1000]{1,2,0:T(8,128)(2,1)} async-done(((bf16[1,512,1000]{1,2,0:T(8,128)(2,1)}), bf16[8,512,1000]{1,2,0:T(8,128)(2,1)}) %all-gather.6.cloned.1.call-update) | async-done | bytes 8192016 | tf_op jit(solution)/shard_map/all_gather | solution.py:39
  404.5 5.8 reduce_sum.39
  410.3 2.3 copy.21
  416.3 46.1 %while.32 = (s32[]{:T(128)}, f32[512]{0:T(512)S(1)}, f32[512]{0:T(512)}, f32[512]{0:T(512)}, f32[512]{0:T(512)}, /*index=5*/f32[512]{0:T(512)}, bf16[4,1024,1000...) while((s32[]{:T(128)}, f32[512]{0:T(512)S(1)}, ...), condition=%wide.region_8.9_spmd.clone, body=%wide.region_2.8_spmd.clone.sunk | while | flops 1187518464 | bytes 12046677 | solution.py:76
  416.3 5.1 fusion.51
  421.4 2.0 fusion.52
  424.8 2.4 multiply_reduce_fusion.2
  427.9 5.1 fusion.51
  432.9 2.0 fusion.52
  436.3 2.4 multiply_reduce_fusion.2
  439.4 5.1 fusion.51
  444.5 2.0 fusion.52
  447.8 2.4 multiply_reduce_fusion.2
  450.9 5.1 fusion.51
  456.0 2.0 fusion.52
  459.4 2.4 multiply_reduce_fusion.2
  462.5 14.5 %all-reduce.1 = (f32[512]{0:T(512)}, f32[512]{0:T(512)}) all-reduce(f32[512]{0:T(512)} %get-tuple-element.120, f32[512]{0:T(512)S(1)} %get-tuple-element.118), channel_id=1, replica_groups=mesh['query'=32,'entity'=8] {'entity'}, use_global_device_ids=true, to_apply=%region_12.13 | all-reduce | flops 1024 | bytes 8192 | tf_op jit(solution)/shard_map/pmax | solution.py:80
  477.7 14.7 %all-reduce = (f32[512]{0:T(512)S(1)}, f32[512]{0:T(512)}, f32[512]{0:T(512)}) all-reduce(f32[512]{0:T(512)S(1)} %get-tuple-element.259, f32[512]{0:T(512)S(1)} %get-tuple-element.257, f32[512]{0:T(512)S(1)} %get-tuple-element.256), channel_id=1, replica_groups=mesh['query'=32,'entity'=8] {'entity'}, use_global_device_ids=true, to_apply=%region_13.14 | all-reduce | flops 1536 | bytes 12288 | tf_op jit(solution)/shard_map/psum | solution.py:83
  492.3 26.0 %while.33 = (s32[]{:T(128)}, f32[512,128]{1,0:T(8,128)S(1)}, f32[4,1024,128]{2,1,0:T(8,128)}, bf16[4,1024,128]{2,1,0:T(8,128)(2,1)}, bf16[512,128]{1,0:T(8,128)(...) while((s32[]{:T(128)}, f32[512,128]{1,0:T(8,128)S(1)}, ...), condition=%wide.region_15.16_spmd.clone, body=%wide.region_14.15_spmd.clone.sunk | while | flops 1454505984 | bytes 16531671 | solution.py:100
  492.3 3.2 fusion.62
  498.9 3.2 fusion.62
  505.4 3.2 fusion.62
  511.9 3.2 fusion.62
  521.0 70.9 %all-reduce.7.cloned.1.call-done = f32[512,128]{1,0:T(8,128)} async-done(((f32[512,128]{1,0:T(8,128)}), f32[512,128]{1,0:T(8,128)}) %all-reduce.7.cloned.1.call-update) | async-done | bytes 262160 | tf_op jit(solution)/shard_map/psum | solution.py:103
  591.9 232.7 %reduce-scatter.2.cloned.1.call-done = f32[128,128]{1,0:T(8,128)} async-done(((f32[4096,128]{1,0:T(8,128)}), f32[128,128]{1,0:T(8,128)}) %reduce-scatter.2.cloned.1.call-update) | async-done | bytes 65552 | tf_op jit(solution)/shard_map/reduce_scatter | solution.py:102
  (161 shorter events, 42.7 us)
Async XLA Ops:
  7.2 269.9 %copy-start = (bf16[4131,128]{1,0:T(8,128)(2,1)S(1)}, bf16[4131,128]{1,0:T(8,128)(2,1)}, u32[]{:S(2)}) copy-start(bf16[4131,128]{1,0:T(8,128)(2,1)} %param.17) | copy-start | bytes 3172612
  7.2 87.1 %all-gather.8.cloned.1.call-start = ((), (), s32[]{:S(2)}) async-start(), calls=%async_computation.3 | async-start | bytes 1081344 | tf_op jit(solution)/shard_map/all_gather | solution.py:30
  7.9 239.5 %all-gather.4.cloned.1.call-start = ((), (), s32[]{:S(2)}) async-start(), calls=%async_computation.1 | async-start | bytes 8650752 | tf_op jit(solution)/shard_map/all_gather | solution.py:29
  9.8 303.0 %all-reduce.5.cloned.1.call-start = ((), (), s32[]{:S(2)}) async-start(), calls=%async_computation.4 | async-start | bytes 262144 | tf_op jit(solution)/shard_map/psum | solution.py:42
  97.6 307.0 %all-gather.6.cloned.1.call-start = ((), (), s32[]{:S(2)}) async-start(), calls=%async_computation.2 | async-start | bytes 9216000 | tf_op jit(solution)/shard_map/all_gather | solution.py:39
  256.5 335.4 %all-reduce.7.cloned.1.call-start = ((), (), s32[]{:S(2)}) async-start(), calls=%async_computation.6 | async-start | bytes 524288 | tf_op jit(solution)/shard_map/psum | solution.py:103
  256.8 12.3 %copy-start.12 = (s32[512]{0:T(512)S(1)}, s32[512]{0:T(512)}, u32[]{:S(2)}) copy-start(s32[512]{0:T(512)} %param.12) | copy-start | bytes 6148
  269.0 9.4 %copy-start.13 = (s32[512]{0:T(512)S(1)}, s32[512]{0:T(512)}, u32[]{:S(2)}) copy-start(s32[512]{0:T(512)} %param.13) | copy-start | bytes 6148
  279.9 33.9 %copy-start.10 = (f32[512]{0:T(512)S(1)}, f32[512]{0:T(512)}, u32[]{:S(2)}) copy-start(f32[512]{0:T(512)} %add_convert_fusion.2) | copy-start | bytes 6148
  424.8 2.4 copy-start.3
  424.8 2.4 copy-start.4
  424.8 2.4 copy-start.6
  424.8 2.4 copy-start.8
  436.3 2.4 copy-start.4
  436.3 2.4 copy-start.6
  436.3 2.4 copy-start.8
  447.8 2.4 copy-start.3
  447.8 2.4 copy-start.4
  447.8 2.4 copy-start.6
  447.8 2.4 copy-start.8
  459.4 2.4 copy-start.4
  459.4 2.4 copy-start.6
  459.4 2.4 copy-start.8
  492.3 3.2 copy-start.1
  492.3 3.2 copy-start.14
  498.9 3.2 copy-start.1
  498.9 3.2 copy-start.14
  505.4 3.2 copy-start.1
  505.4 3.2 copy-start.14
  511.9 3.2 copy-start.1
  511.9 3.2 copy-start.14
  519.1 305.5 %reduce-scatter.2.cloned.1.call-start = ((), (), s32[]{:S(2)}) async-start(), calls=%async_computation.5 | async-start | bytes 2162688 | tf_op jit(solution)/shard_map/reduce_scatter | solution.py:102
  (18 other events, 17.2 us)
Sparse Core Ops, SparseCore 0:
  11.4 82.7 all-gather.7
  98.4 149.0 all-gather.3
  250.1 62.7 all-reduce.4
  314.6 89.8 all-gather.5
  519.2 72.6 all-reduce.6
  594.8 229.7 reduce-scatter.1
